TPU v7x, 512 devices: a whole 4x4x16 slice. The times are simulated.
512 devices in a mesh: blk: 512 (over x, y, z, core).
Axes of the slice: x: 4, y: 4, z: 16, core: 2. Of those that a mesh axis runs over, the one named last changes fastest.
Arguments:
- points: float32 [786432, 128], P('blk'), may hold values from -6 to 6
- inv_scale: float32 [128], replicated, may hold values from 0.03 to 0.3
- vectors: float32 [786432, 64], P('blk'), may hold values from -6 to 6
Outputs:
- product: float32 [786432, 64], P('blk')
All inputs are finite; a program needn't handle non-finite values.
Results may differ from a plain program's by a relative error of at most 0.0003.
Values sent between devices are 32-bit elements; how exact they have to be, the bound alone decides.
No kernel may reach another device: no remote copies, remote signals or barrier semaphores. Data moves between devices by JAX's collectives and lax.ppermute only.
A program may use at most 64 MiB of HBM per device.

v0:
```python
import math

import jax
import jax.numpy as jnp
from jax import lax
from jax.experimental import pallas as pl
from jax.experimental.pallas import tpu as pltpu
from jax.sharding import PartitionSpec as P

F32, BF16 = jnp.float32, jnp.bfloat16
SUBLANES, LANES = 8, 128
WIDTH = 768
VMEM_LIMIT = 24 * 2**20
SELF_FLOPS = 10**9
VISIT_FLOPS = 10**10
ROOT_LOG2E = math.sqrt(math.log2(math.e))


def dot(a, b, contract_b=0):
    dims = (((1,), (contract_b,)), ((), ()))
    return lax.dot_general(a, b, dims, preferred_element_type=F32)


def split(x):
    high = x.astype(BF16)
    return high, (x - high.astype(F32)).astype(BF16)


def split_points(points, gain):
    scaled = points * (gain * ROOT_LOG2E)
    high, low = split(scaled)
    h, l = high.astype(F32), low.astype(F32)
    half = -0.5 * jnp.sum(h * (h + 2.0 * l), axis=1, keepdims=True)
    first = half.astype(BF16).astype(F32)
    second = (half - first).astype(BF16).astype(F32)
    third = half - first - second
    return high, low, (first, second, third)


def place(parts, ones_at, parts_at, shape):
    lane = lax.broadcasted_iota(jnp.int32, shape, 1)
    out = jnp.where((lane >= ones_at) & (lane < ones_at + 3), 1.0, 0.0)
    for at, part in enumerate(parts):
        out = jnp.where(lane == parts_at + at, part, out)
    return out.astype(BF16)


def row_factor(points, gain):
    high, low, parts = split_points(points, gain)
    sq = place(parts, 3, 0, (points.shape[0], LANES))
    return jnp.concatenate([high, low, high, sq], axis=1)


def column_factor(points, gain):
    high, low, parts = split_points(points, gain)
    sq = place(parts, 0, 3, (points.shape[0], LANES))
    return jnp.concatenate([high, high, low, sq], axis=1)


def split_vectors(vec_t):
    return jnp.concatenate(split(vec_t), axis=0)


def apply_strip(tile_high, tile_low, vec, rhs):
    both = dot(vec, tile_high)
    return both[:rhs] + both[rhs:] + dot(vec[:rhs], tile_low)


def tile_strip(rows, column):
    return split(jnp.exp2(dot(rows, column, 1)))


def strips(points):
    return [slice(at, at + WIDTH) for at in range(0, points, WIDTH)]


def unpack_vectors(packed, rhs, points):
    rows = range(points, points + rhs * points // LANES, rhs)
    return jnp.concatenate([packed[at : at + rhs, :] for at in rows], axis=1)


def unpack_gain(packed):
    end = packed.shape[0] - SUBLANES
    return packed[end : end + 1, :]


def self_kernel(pts, vec_t, gain, out, packed, vec_out):
    rhs, points = vec_t.shape
    packed[:points, :] = pts[...]
    for at in range(points // LANES):
        rows = slice(points + at * rhs, points + (at + 1) * rhs)
        packed[rows, :] = vec_t[:, at * LANES : (at + 1) * LANES]
    end = points + rhs * points // LANES
    packed[end:, :] = jnp.broadcast_to(gain[...], (SUBLANES, LANES))
    vec_out[...] = vec_t[...]
    column = column_factor(pts[...], gain[...])
    rows = row_factor(pts[...], gain[...])
    vec = split_vectors(vec_t[...])
    for at in strips(points):
        high, low = tile_strip(rows, column[at, :])
        out[:, at] = apply_strip(high, low, vec, rhs)


def from_columns(high, low, column_vec, rhs):
    both = dot(high, column_vec)
    return both[:, :rhs] + both[:, rhs:] + dot(low, column_vec[:, :rhs])


def column_vectors(vec_t):
    return jnp.concatenate(split(vec_t.T), axis=1)


def visit_kernel(other, own, back, tile_high, tile_low):
    rhs, points = back.shape
    vec = column_vectors(unpack_vectors(own, rhs, points))
    column = column_factor(own[:points, :], unpack_gain(own))
    rows = row_factor(other[...], unpack_gain(own))
    partial = None
    for at in strips(points):
        high, low = tile_strip(rows, column[at, :])
        tile_high[:, at] = high
        tile_low[:, at] = low
        added = from_columns(high, low, vec[at, :], rhs)
        partial = added if partial is None else partial + added
    back[...] = partial.T


def mate_kernel(core, mate, other, other_vec, own, total, partial, out, back, for_mate):
    rhs, points = total.shape
    first = core[0] == 0
    gain = unpack_gain(own)
    column = column_factor(mate[:points, :], gain)
    mate_vec = column_vectors(unpack_vectors(mate, rhs, points))
    rows = row_factor(jnp.where(first, other[...], own[:points, :]), gain)
    own_vec = unpack_vectors(own, rhs, points)
    row_vec = split_vectors(jnp.where(first, other_vec[...], own_vec))
    gained = None
    for at in strips(points):
        high, low = tile_strip(rows, column[at, :])
        for_mate[:, at] = apply_strip(high, low, row_vec, rhs)
        added = from_columns(high, low, mate_vec[at, :], rhs)
        gained = added if gained is None else gained + added
    gained = gained.T
    back[...] = partial[...] + jnp.where(first, gained, 0.0)
    out[...] = total[...] + jnp.where(first, 0.0, gained)


def apply_kernel(tile_high, tile_low, vec_t, total, out):
    rhs, points = total.shape
    vec = split_vectors(vec_t[...])
    for at in strips(points):
        out[:, at] = total[:, at] + apply_strip(tile_high[:, at], tile_low[:, at], vec, rhs)


def per_device(points, inv_scale, vectors):
    rows, features = points.shape
    rhs = vectors.shape[1]
    n = lax.axis_size("blk")
    ahead = [(i, (i - 2) % n if i % 2 == 0 else (i + 2) % n) for i in range(n)]
    back_home = [(d, s) for s, d in ahead]
    swap = [(i, i ^ 1) for i in range(n)]
    scalar, whole = [pl.BlockSpec(memory_space=space) for space in (pltpu.SMEM, pltpu.VMEM)]

    def call(kernel, outs, specs, *args, flops=1000, vmem=VMEM_LIMIT):
        return pl.pallas_call(
            kernel,
            out_shape=outs,
            in_specs=specs,
            compiler_params=pltpu.CompilerParams(vmem_limit_bytes=vmem),
            cost_estimate=pl.CostEstimate(
                flops=flops, bytes_accessed=rows, transcendentals=rows
            ),
        )(*args)

    core = (lax.axis_index("blk") % 2)[None]
    gain = inv_scale[None, :]
    vec_t = vectors.T
    product = jax.ShapeDtypeStruct((rhs, rows), F32)
    tile = jax.ShapeDtypeStruct((rows, rows), BF16)
    packed = jax.ShapeDtypeStruct((rows + rhs * rows // LANES + SUBLANES, LANES), F32)

    visitor = lax.ppermute(points, "blk", ahead)
    total, own, vec_copy = call(
        self_kernel, (product, packed, product), [whole] * 3, points, vec_t, gain, flops=SELF_FLOPS
    )
    mate = lax.ppermute(own, "blk", swap)
    visitor_vec = lax.ppermute(vec_copy, "blk", ahead)
    partial, high, low = call(
        visit_kernel,
        (product, tile, tile),
        [whole] * 2,
        *(visitor, own),
        flops=VISIT_FLOPS,
    )
    total, partial, for_mate = call(
        mate_kernel,
        (product, product, product),
        [scalar] + [whole] * 6,
        *(core, mate, visitor, visitor_vec, own, total, partial),
        flops=SELF_FLOPS,
    )
    returned = lax.ppermute(partial, "blk", back_home)
    from_chip = lax.ppermute(for_mate, "blk", swap)
    total = call(apply_kernel, product, [whole] * 4, high, low, visitor_vec, total)
    return (total + returned + from_chip).T


def solution(mesh):
    in_specs = (P("blk", None), P(), P("blk", None))
    out_specs = P("blk", None)
    return jax.shard_map(
        per_device, mesh=mesh, in_specs=in_specs, out_specs=out_specs, check_vma=False
    )
```

profile of v0, /device:TPU:1, one launch (start us, length us, event | category | flops | bytes accessed | tf_op | source)
XLA Modules:
  0.0 59.3 jit_solution(10721857826778872310)
XLA Ops:
  0.0 4.4 %collective-permute-start = (f32[1536,128]{1,0:T(8,128)}, f32[1536,128]{1,0:T(8,128)S(1)}, u32[]{:S(2)}, u32[]{:S(2)}) collective-permute-start(f32[1536,128]{1,0:T(8,128)} %pts.1), channel_id=1, source_target_pairs={{0,510},{1,3},{2,0},{3,5},{4,2},{5,7},{6,4},{7,9},{8,6},{9,11},{10... | collective-permute-start | bytes 2359304 | tf_op jit(solution)/shard_map/ppermute | solution.py:182
  4.4 0.0 copy-start.2
  4.4 1.1 %copy-done.2 = f32[1536,128]{1,0:T(8,128)S(1)} copy-done((f32[1536,128]{1,0:T(8,128)S(1)}, f32[1536,128]{1,0:T(8,128)}, u32[]{:S(2)}) %copy-start.2) | copy-done | bytes 786456
  5.5 0.0 copy-start.3
  5.5 1.0 %copy-done.3 = f32[1536,64]{0,1:T(8,128)S(1)} copy-done((f32[1536,64]{0,1:T(8,128)S(1)}, f32[1536,64]{0,1:T(8,128)}, u32[]{:S(2)}) %copy-start.3) | copy-done | bytes 393240
  6.5 0.0 copy-start.4
  6.5 0.7 %copy-done.4 = f32[128]{0:T(128)S(1)} copy-done((f32[128]{0:T(128)S(1)}, f32[128]{0:T(128)}, u32[]{:S(2)}) %copy-start.4) | copy-done | bytes 536
  7.2 5.3 %shard_map.37 = (f32[64,1536]{1,0:T(8,128)S(1)}, f32[2312,128]{1,0:T(8,128)S(1)}, f32[64,1536]{1,0:T(8,128)}) custom-call(f32[1536,128]{1,0:T(8,128)S(1)} %copy-done.2, f32[64,1536]{1,0:T(8,128)S(1)} %bitcast.5, f32[1,128]{1,0:T(1,128)S(1)} %bitcast.6), custom_call_target="tpu_custom_call" | custom-call | flops 1000000000 | bytes 1536 | tf_op jit(solution)/shard_map/pallas_call | solution.py:165
  12.5 0.0 copy-start
  12.5 0.7 %copy-done = f32[64,1536]{1,0:T(8,128)} copy-done((f32[64,1536]{1,0:T(8,128)}, f32[64,1536]{1,0:T(8,128)S(1)}, u32[]{:S(2)}) %copy-start) | copy-done | bytes 393240
  13.2 15.1 %collective-permute-start.2 = (f32[2312,128]{1,0:T(8,128)S(1)}, f32[2312,128]{1,0:T(8,128)S(1)}, u32[]{:S(2)}, u32[]{:S(2)}) collective-permute-start(f32[2312,128]{1,0:T(8,128)S(1)} %get-tuple-element.14.own), channel_id=1, source_target_pairs={{0,1},{1,0},{2,3},{3,2},{4,5},{5,4},{6,7},{7,6},{8,9},{9,8},{10,11... | collective-permute-start | bytes 3551240 | tf_op jit(solution)/shard_map/ppermute | solution.py:186
  28.3 2.1 %collective-permute-start.1 = (f32[64,1536]{1,0:T(8,128)}, f32[64,1536]{1,0:T(8,128)S(1)}, u32[]{:S(2)}, u32[]{:S(2)}) collective-permute-start(f32[64,1536]{1,0:T(8,128)} %get-tuple-element.17), channel_id=1, source_target_pairs={{0,510},{1,3},{2,0},{3,5},{4,2},{5,7},{6,4},{7,9},{8,6},{9,11},{10... | collective-permute-start | bytes 1179656 | tf_op jit(solution)/shard_map/ppermute | solution.py:187
  30.4 0.0 copy-start.1
  30.4 0.0 collective-permute-done.other
  30.4 6.8 %shard_map.38 = (f32[64,1536]{1,0:T(8,128)S(1)}, bf16[1536,1536]{1,0:T(8,128)(2,1)S(1)}, bf16[1536,1536]{1,0:T(8,128)(2,1)S(1)}) custom-call(f32[1536,128]{1,0:T(8,128)S(1)} %collective-permute-done.other, f32[2312,128]{1,0:T(8,128)S(1)} %get-tuple-element.14.own), custom_call_target="tpu_custom_call" | custom-call | flops 10000000000 | bytes 1536 | tf_op jit(solution)/shard_map/pallas_call | solution.py:165
  37.2 5.3 %collective-permute-done.1.other_vec.vec_t = f32[64,1536]{1,0:T(8,128)S(1)} collective-permute-done((f32[64,1536]{1,0:T(8,128)}, f32[64,1536]{1,0:T(8,128)S(1)}, u32[]{:S(2)}, u32[]{:S(2)}) %collective-permute-start.1) | collective-permute-done | bytes 393248 | tf_op jit(solution)/shard_map/ppermute | solution.py:187
  42.4 0.0 collective-permute-done.2.mate
  42.4 0.0 copy-done.1
  42.5 7.2 %shard_map.39 = (f32[64,1536]{1,0:T(8,128)S(1)}, f32[64,1536]{1,0:T(8,128)S(1)}, f32[64,1536]{1,0:T(8,128)S(1)}) custom-call(s32[1]{0:T(128)} %bitcast.2.core, f32[2312,128]{1,0:T(8,128)S(1)} %collective-permute-done.2.mate, f32[1536,128]{1,0:T(8,128)S(1)} %collective-permute-done.other, f32[64,1536]{1,0:T(8,128)S(1)} %collective-permute-done.1.other_vec.vec_t, ...), custom_call_target="tpu_custom_call" | custom-call | flops 1000000000 | bytes 1536 | tf_op jit(solution)/shard_map/pallas_call | solution.py:165
  49.7 3.6 %collective-permute-start.3 = (f32[64,1536]{1,0:T(8,128)S(1)}, f32[64,1536]{1,0:T(8,128)S(1)}, u32[]{:S(2)}, u32[]{:S(2)}) collective-permute-start(f32[64,1536]{1,0:T(8,128)S(1)} %get-tuple-element.21), channel_id=1, source_target_pairs={{510,0},{3,1},{0,2},{5,3},{2,4},{7,5},{4,6},{9,7},{6,8},{11,9},{8,... | collective-permute-start | bytes 1179656 | tf_op jit(solution)/shard_map/ppermute | solution.py:202
  53.3 1.9 %collective-permute-start.4 = (f32[64,1536]{1,0:T(8,128)S(1)}, f32[64,1536]{1,0:T(8,128)S(1)}, u32[]{:S(2)}, u32[]{:S(2)}) collective-permute-start(f32[64,1536]{1,0:T(8,128)S(1)} %get-tuple-element.22), channel_id=1, source_target_pairs={{0,1},{1,0},{2,3},{3,2},{4,5},{5,4},{6,7},{7,6},{8,9},{9,8},{10,11... | collective-permute-start | bytes 1179656 | tf_op jit(solution)/shard_map/ppermute | solution.py:203
  55.2 1.6 %shard_map.40 = f32[64,1536]{1,0:T(8,128)S(1)} custom-call(bf16[1536,1536]{1,0:T(8,128)(2,1)S(1)} %get-tuple-element.15.tile_high, bf16[1536,1536]{1,0:T(8,128)(2,1)S(1)} %get-tuple-element.16.tile_low, f32[64,1536]{1,0:T(8,128)S(1)} %collective-permute-done.1.other_vec.vec_t, f32[64,1536]{1,0:T(8,128)S(1)} %get-tuple-element.20.total), custom_call_target="tpu_custom_call" | custom-call | flops 1000 | bytes 1536 | tf_op jit(solution)/shard_map/pallas_call | solution.py:165
  56.8 1.7 %collective-permute-done.3 = f32[64,1536]{1,0:T(8,128)S(1)} collective-permute-done((f32[64,1536]{1,0:T(8,128)S(1)}, f32[64,1536]{1,0:T(8,128)S(1)}, u32[]{:S(2)}, u32[]{:S(2)}) %collective-permute-start.3) | collective-permute-done | bytes 393248 | tf_op jit(solution)/shard_map/ppermute | solution.py:202
  58.5 0.0 collective-permute-done.4
  58.5 0.8 %add_bitcast_fusion = f32[1536,64]{0,1:T(8,128)} fusion(f32[64,1536]{1,0:T(8,128)S(1)} %collective-permute-done.4, f32[64,1536]{1,0:T(8,128)S(1)} %shard_map.40, f32[64,1536]{1,0:T(8,128)S(1)} %collective-permute-done.3), kind=kLoop, calls=%fused_computation | loop fusion | flops 196608 | bytes 1572864 | tf_op jit(solution)/shard_map/transpose | solution.py:205
Async XLA Ops:
  0.0 30.4 %collective-permute-start = (f32[1536,128]{1,0:T(8,128)}, f32[1536,128]{1,0:T(8,128)S(1)}, u32[]{:S(2)}, u32[]{:S(2)}) collective-permute-start(f32[1536,128]{1,0:T(8,128)} %pts.1), channel_id=1, source_target_pairs={{0,510},{1,3},{2,0},{3,5},{4,2},{5,7},{6,4},{7,9},{8,6},{9,11},{10... | collective-permute-start | bytes 2359304 | tf_op jit(solution)/shard_map/ppermute | solution.py:182
  4.4 1.1 %copy-start.2 = (f32[1536,128]{1,0:T(8,128)S(1)}, f32[1536,128]{1,0:T(8,128)}, u32[]{:S(2)}) copy-start(f32[1536,128]{1,0:T(8,128)} %pts.1) | copy-start | bytes 2359300
  5.5 1.0 %copy-start.3 = (f32[1536,64]{0,1:T(8,128)S(1)}, f32[1536,64]{0,1:T(8,128)}, u32[]{:S(2)}) copy-start(f32[1536,64]{0,1:T(8,128)} %param.5) | copy-start | bytes 1179652
  6.5 0.7 %copy-start.4 = (f32[128]{0:T(128)S(1)}, f32[128]{0:T(128)}, u32[]{:S(2)}) copy-start(f32[128]{0:T(128)} %param.4) | copy-start | bytes 1540
  12.5 0.7 %copy-start = (f32[64,1536]{1,0:T(8,128)}, f32[64,1536]{1,0:T(8,128)S(1)}, u32[]{:S(2)}) copy-start(f32[64,1536]{1,0:T(8,128)S(1)} %get-tuple-element.18.total) | copy-start | bytes 1179652
  13.2 29.2 %collective-permute-start.2 = (f32[2312,128]{1,0:T(8,128)S(1)}, f32[2312,128]{1,0:T(8,128)S(1)}, u32[]{:S(2)}, u32[]{:S(2)}) collective-permute-start(f32[2312,128]{1,0:T(8,128)S(1)} %get-tuple-element.14.own), channel_id=1, source_target_pairs={{0,1},{1,0},{2,3},{3,2},{4,5},{5,4},{6,7},{7,6},{8,9},{9,8},{10,11... | collective-permute-start | bytes 3551240 | tf_op jit(solution)/shard_map/ppermute | solution.py:186
  28.3 14.2 %collective-permute-start.1 = (f32[64,1536]{1,0:T(8,128)}, f32[64,1536]{1,0:T(8,128)S(1)}, u32[]{:S(2)}, u32[]{:S(2)}) collective-permute-start(f32[64,1536]{1,0:T(8,128)} %get-tuple-element.17), channel_id=1, source_target_pairs={{0,510},{1,3},{2,0},{3,5},{4,2},{5,7},{6,4},{7,9},{8,6},{9,11},{10... | collective-permute-start | bytes 1179656 | tf_op jit(solution)/shard_map/ppermute | solution.py:187
  30.4 12.0 %copy-start.1 = (f32[64,1536]{1,0:T(8,128)S(1)}, f32[64,1536]{1,0:T(8,128)}, u32[]{:S(2)}) copy-start(f32[64,1536]{1,0:T(8,128)} %copy-done) | copy-start | bytes 1179652
  49.7 8.8 %collective-permute-start.3 = (f32[64,1536]{1,0:T(8,128)S(1)}, f32[64,1536]{1,0:T(8,128)S(1)}, u32[]{:S(2)}, u32[]{:S(2)}) collective-permute-start(f32[64,1536]{1,0:T(8,128)S(1)} %get-tuple-element.21), channel_id=1, source_target_pairs={{510,0},{3,1},{0,2},{5,3},{2,4},{7,5},{4,6},{9,7},{6,8},{11,9},{8,... | collective-permute-start | bytes 1179656 | tf_op jit(solution)/shard_map/ppermute | solution.py:202
  53.3 5.2 %collective-permute-start.4 = (f32[64,1536]{1,0:T(8,128)S(1)}, f32[64,1536]{1,0:T(8,128)S(1)}, u32[]{:S(2)}, u32[]{:S(2)}) collective-permute-start(f32[64,1536]{1,0:T(8,128)S(1)} %get-tuple-element.22), channel_id=1, source_target_pairs={{0,1},{1,0},{2,3},{3,2},{4,5},{5,4},{6,7},{7,6},{8,9},{9,8},{10,11... | collective-permute-start | bytes 1179656 | tf_op jit(solution)/shard_map/ppermute | solution.py:203
where the time goes:
time: 59.6 us; the launch traced here: 59.3 us
  starting transfers between devices  27 us (45%)
  Pallas kernels  20.9 us (35%)
  waiting for transfers between devices  6.97 us (12%)
  local copies, waits for them, and re-layouts  3.53 us (6%)
  other arithmetic  0.81 us (1%)
    pallas_call x4, Pallas kernels, call(): pl.pallas_call(kernel, out_shape=outs, in_specs=specs, compiler_params=pl...  20.9 us
    ppermute x1, starting transfers between devices, per_device(): mate = lax.ppermute(own, 'blk', swap)  15.1 us
    ppermute x1, waiting for transfers between devices, per_device(): visitor_vec = lax.ppermute(vec_copy, 'blk', ahead)  5.26 us
    ppermute x1, starting transfers between devices, per_device(): visitor = lax.ppermute(points, 'blk', ahead)  4.36 us
    ppermute x1, starting transfers between devices, per_device(): returned = lax.ppermute(partial, 'blk', back_home)  3.56 us
    unnamed x10, local copies, waits for them, and re-layouts  3.53 us
    ppermute x1, starting transfers between devices, per_device(): visitor_vec = lax.ppermute(vec_copy, 'blk', ahead)  2.1 us
    ppermute x1, starting transfers between devices, per_device(): from_chip = lax.ppermute(for_mate, 'blk', swap)  1.92 us
  transfers between devices with their start and end apart: 5, of which 2 were waited for; matrix products, arithmetic and copies ran while one was open for 0% of the time, Pallas kernels for 23%

commit v1 on v0

v1 whole, which is shorter than its diff:
```python
import math

import jax
import jax.numpy as jnp
from jax import lax
from jax.experimental import pallas as pl
from jax.experimental.pallas import tpu as pltpu
from jax.sharding import PartitionSpec as P

F32, BF16 = jnp.float32, jnp.bfloat16
SUBLANES, LANES = 8, 128
WIDTH = 768
VMEM_LIMIT = 24 * 2**20
SELF_FLOPS = 10**9
VISIT_FLOPS = 10**10
ROOT_LOG2E = math.sqrt(math.log2(math.e))


def dot(a, b, contract_b=0):
    dims = (((1,), (contract_b,)), ((), ()))
    return lax.dot_general(a, b, dims, preferred_element_type=F32)


def split(x):
    high = x.astype(BF16)
    return high, (x - high.astype(F32)).astype(BF16)


def split_points(points, gain):
    scaled = points * (gain * ROOT_LOG2E)
    high, low = split(scaled)
    h, l = high.astype(F32), low.astype(F32)
    half = -0.5 * jnp.sum(h * (h + 2.0 * l), axis=1, keepdims=True)
    first = half.astype(BF16).astype(F32)
    second = (half - first).astype(BF16).astype(F32)
    third = half - first - second
    return high, low, (first, second, third)


def place(parts, ones_at, parts_at, points, lane):
    ones = jnp.where((lane >= ones_at) & (lane < ones_at + 3), 1.0, 0.0)
    out = jnp.broadcast_to(ones, (points, LANES))
    for at, part in enumerate(parts):
        out = jnp.where(lane == parts_at + at, part, out)
    return out.astype(BF16)


def lanes():
    return lax.broadcasted_iota(jnp.int32, (1, LANES), 1)


def row_factor(points, gain, lane=None):
    high, low, parts = split_points(points, gain)
    sq = place(parts, 3, 0, points.shape[0], lanes() if lane is None else lane)
    return jnp.concatenate([high, low, high, sq], axis=1)


def column_factor(points, gain, lane=None):
    high, low, parts = split_points(points, gain)
    sq = place(parts, 0, 3, points.shape[0], lanes() if lane is None else lane)
    return jnp.concatenate([high, high, low, sq], axis=1)


def split_vectors(vec_t):
    return jnp.concatenate(split(vec_t), axis=0)


def apply_strip(tile_high, tile_low, vec, rhs):
    both = dot(vec, tile_high)
    return both[:rhs] + both[rhs:] + dot(vec[:rhs], tile_low)


def tile_strip(rows, column):
    return split(jnp.exp2(dot(rows, column, 1)))


def strips(points):
    return [slice(at, at + WIDTH) for at in range(0, points, WIDTH)]


def unpack_vectors(packed, rhs, points):
    rows = range(points, points + rhs * points // LANES, rhs)
    return jnp.concatenate([packed[at : at + rhs, :] for at in rows], axis=1)


def unpack_gain(packed):
    end = packed.shape[0] - SUBLANES
    return packed[end : end + 1, :]


def lane_kernel(out):
    out[...] = lax.broadcasted_iota(jnp.int32, out.shape, 1)


def self_kernel(lane, pts, vec_t, gain, out, packed, vec_out):
    rhs, points = vec_t.shape
    packed[:points, :] = pts[...]
    for at in range(points // LANES):
        rows = slice(points + at * rhs, points + (at + 1) * rhs)
        packed[rows, :] = vec_t[:, at * LANES : (at + 1) * LANES]
    end = points + rhs * points // LANES
    packed[end:, :] = jnp.broadcast_to(gain[...], (SUBLANES, LANES))
    vec_out[...] = vec_t[...]
    column = column_factor(pts[...], gain[...], lane[:1, :])
    rows = row_factor(pts[...], gain[...], lane[:1, :])
    vec = split_vectors(vec_t[...])
    for at in strips(points):
        high, low = tile_strip(rows, column[at, :])
        out[:, at] = apply_strip(high, low, vec, rhs)


def from_columns(high, low, column_vec, rhs):
    both = dot(high, column_vec)
    return both[:, :rhs] + both[:, rhs:] + dot(low, column_vec[:, :rhs])


def column_vectors(vec_t):
    return jnp.concatenate(split(vec_t.T), axis=1)


def visit_kernel(other, own, back, tile_high, tile_low):
    rhs, points = back.shape
    gain = unpack_gain(own)
    vec = column_vectors(unpack_vectors(own, rhs, points))
    column = column_factor(own[:points, :], gain)
    rows = row_factor(other[...], gain)
    partial = None
    for at in strips(points):
        high, low = tile_strip(rows, column[at, :])
        tile_high[:, at] = high
        tile_low[:, at] = low
        added = from_columns(high, low, vec[at, :], rhs)
        partial = added if partial is None else partial + added
    back[...] = partial.T


def mate_kernel(other, mate, partial, back):
    rhs, points = back.shape
    gain = unpack_gain(mate)
    rows = row_factor(mate[:points, :], gain)
    vec = split_vectors(unpack_vectors(mate, rhs, points))
    column = column_factor(other[...], gain)
    for at in strips(points):
        high, low = tile_strip(rows, column[at, :])
        back[:, at] = partial[:, at] + apply_strip(high, low, vec, rhs)


def own_kernel(tile_high, tile_low, other_vec, own, mate, out):
    rhs, points = out.shape
    gain = unpack_gain(own)
    vec = split_vectors(other_vec[...])
    column = column_factor(own[:points, :], gain)
    rows = row_factor(mate[:points, :], gain)
    mate_vec = split_vectors(unpack_vectors(mate, rhs, points))
    for at in strips(points):
        gained = apply_strip(tile_high[:, at], tile_low[:, at], vec, rhs)
        high, low = tile_strip(rows, column[at, :])
        out[:, at] = gained + apply_strip(high, low, mate_vec, rhs)


def per_device(points, inv_scale, vectors):
    rows, features = points.shape
    rhs = vectors.shape[1]
    n = lax.axis_size("blk")
    ahead = [(i, (i - 2) % n if i % 2 == 0 else (i + 2) % n) for i in range(n)]
    back_home = [(d, s) for s, d in ahead]
    swap = [(i, i ^ 1) for i in range(n)]
    def call(kernel, outs, *args, flops):
        return pl.pallas_call(
            kernel,
            out_shape=outs,
            compiler_params=pltpu.CompilerParams(vmem_limit_bytes=VMEM_LIMIT),
            cost_estimate=pl.CostEstimate(
                flops=flops, bytes_accessed=rows, transcendentals=rows
            ),
        )(*args)

    gain = inv_scale[None, :]
    vec_t = vectors.T
    product = jax.ShapeDtypeStruct((rhs, rows), F32)
    tile = jax.ShapeDtypeStruct((rows, rows), BF16)
    packed = jax.ShapeDtypeStruct((rows + rhs * rows // LANES + SUBLANES, LANES), F32)

    visitor = lax.ppermute(points, "blk", ahead)
    lane_shape = jax.ShapeDtypeStruct((SUBLANES, LANES), jnp.int32)
    lane = call(lane_kernel, lane_shape, flops=VISIT_FLOPS)
    total, own, vec_copy = call(
        self_kernel,
        (product, packed, product),
        *(lane, points, vec_t, gain),
        flops=SELF_FLOPS,
    )
    mate = lax.ppermute(own, "blk", swap)
    visitor_vec = lax.ppermute(vec_copy, "blk", ahead)
    partial, high, low = call(
        visit_kernel, (product, tile, tile), visitor, own, flops=VISIT_FLOPS
    )
    partial = call(mate_kernel, product, visitor, mate, partial, flops=SELF_FLOPS)
    returned = lax.ppermute(partial, "blk", back_home)
    gained = call(own_kernel, product, high, low, visitor_vec, own, mate, flops=SELF_FLOPS)
    return (total + gained + returned).T


def solution(mesh):
    in_specs = (P("blk", None), P(), P("blk", None))
    out_specs = P("blk", None)
    return jax.shard_map(
        per_device, mesh=mesh, in_specs=in_specs, out_specs=out_specs, check_vma=False
    )
```

time: 59.6 us -> 53.7 us (0.901)
  waiting for transfers between devices: 6.97 us -> 0.01 us
  starting transfers between devices: 27 us -> 30.7 us
  local copies, waits for them, and re-layouts: 3.53 us -> 0.01 us
  Pallas kernels: 20.9 us -> 21.9 us
    ppermute x1, starting transfers between devices: 3.56 us -> 9.01 us  [per_device(): returned = lax.ppermute(partial, 'blk', back_home)]
    ppermute x1, waiting for transfers between devices: 5.26 us -> 0.01 us  [per_device(): visitor_vec = lax.ppermute(vec_copy, 'blk', ahead)]
    unnamed x10 -> x6, local copies, waits for them, and re-layouts: 3.53 us -> 0.01 us
    ppermute x1 -> x0, starting transfers between devices: 1.92 us -> none  [per_device(): from_chip = lax.ppermute(for_mate, 'blk', swap)]
    ppermute x1, waiting for transfers between devices: 1.7 us -> 0.01 us  [per_device(): returned = lax.ppermute(partial, 'blk', back_home)]
    pallas_call x4 -> x5, Pallas kernels: 20.9 us -> 21.9 us  [call(): pl.pallas_call(kernel, out_shape=outs, compiler_params=pltpu.CompilerPara...]
  transfers between devices with their start and end apart: 5 -> 4, of which waited for: 2 -> 0; matrix products, arithmetic and copies ran while one was open for 0% -> 0% of each run, Pallas kernels for 23% -> 41%
where the time goes in v1:
time: 53.7 us; the launch traced here: 53.5 us
  starting transfers between devices  30.7 us (57%)
  Pallas kernels  21.9 us (41%)
  other arithmetic  0.83 us (2%)
    pallas_call x5, Pallas kernels, call(): pl.pallas_call(kernel, out_shape=outs, compiler_params=pltpu.CompilerPara...  21.9 us
    ppermute x1, starting transfers between devices, per_device(): mate = lax.ppermute(own, 'blk', swap)  15.1 us
    ppermute x1, starting transfers between devices, per_device(): returned = lax.ppermute(partial, 'blk', back_home)  9.01 us
    ppermute x1, starting transfers between devices, per_device(): visitor = lax.ppermute(points, 'blk', ahead)  4.51 us
    ppermute x1, starting transfers between devices, per_device(): visitor_vec = lax.ppermute(vec_copy, 'blk', ahead)  2.1 us
  transfers between devices with their start and end apart: 4, of which 0 were waited for; matrix products, arithmetic and copies ran while one was open for 0% of the time, Pallas kernels for 41%

profile of v1, /device:TPU:1, one launch (start us, length us, event | category | flops | bytes accessed | tf_op | source)
XLA Modules:
  0.0 53.5 jit_solution(5635736661001543070)
XLA Ops:
  0.0 0.0 copy-start
  0.0 0.0 copy-start.1
  0.0 0.0 copy-start.2
  0.0 4.5 %collective-permute-start = (f32[1536,128]{1,0:T(8,128)}, f32[1536,128]{1,0:T(8,128)S(1)}, u32[]{:S(2)}, u32[]{:S(2)}) collective-permute-start(f32[1536,128]{1,0:T(8,128)} %pts.1), channel_id=1, source_target_pairs={{0,510},{1,3},{2,0},{3,5},{4,2},{5,7},{6,4},{7,9},{8,6},{9,11},{10... | collective-permute-start | bytes 2359304 | tf_op jit(solution)/shard_map/ppermute | solution.py:184
  4.5 0.0 copy-done
  4.5 0.0 copy-done.1
  4.6 0.0 copy-done.2
  4.6 4.7 %shard_map.38 = (f32[64,1536]{1,0:T(8,128)S(1)}, f32[2312,128]{1,0:T(8,128)S(1)}, f32[64,1536]{1,0:T(8,128)S(1)}) custom-call(s32[8,128]{1,0:T(8,128)S(1)} %shard_map.37.lane, f32[1536,128]{1,0:T(8,128)S(1)} %copy-done, f32[64,1536]{1,0:T(8,128)S(1)} %bitcast.4, f32[1,128]{1,0:T(1,128)S(1)} %bitcast.5), custom_call_target="tpu_custom_call" | custom-call | flops 1000000000 | bytes 1536 | tf_op jit(solution)/shard_map/pallas_call | solution.py:169
  9.2 15.1 %collective-permute-start.2 = (f32[2312,128]{1,0:T(8,128)S(1)}, f32[2312,128]{1,0:T(8,128)S(1)}, u32[]{:S(2)}, u32[]{:S(2)}) collective-permute-start(f32[2312,128]{1,0:T(8,128)S(1)} %get-tuple-element.12.own), channel_id=1, source_target_pairs={{0,1},{1,0},{2,3},{3,2},{4,5},{5,4},{6,7},{7,6},{8,9},{9,8},{10,11... | collective-permute-start | bytes 3551240 | tf_op jit(solution)/shard_map/ppermute | solution.py:193
  24.3 2.1 %collective-permute-start.1 = (f32[64,1536]{1,0:T(8,128)S(1)}, f32[64,1536]{1,0:T(8,128)S(1)}, u32[]{:S(2)}, u32[]{:S(2)}) collective-permute-start(f32[64,1536]{1,0:T(8,128)S(1)} %get-tuple-element.15), channel_id=1, source_target_pairs={{0,510},{1,3},{2,0},{3,5},{4,2},{5,7},{6,4},{7,9},{8,6},{9,11},{10... | collective-permute-start | bytes 1179656 | tf_op jit(solution)/shard_map/ppermute | solution.py:194
  26.4 0.0 collective-permute-done.other
  26.4 6.8 %shard_map.39 = (f32[64,1536]{1,0:T(8,128)S(1)}, bf16[1536,1536]{1,0:T(8,128)(2,1)S(1)}, bf16[1536,1536]{1,0:T(8,128)(2,1)S(1)}) custom-call(f32[1536,128]{1,0:T(8,128)S(1)} %collective-permute-done.other, f32[2312,128]{1,0:T(8,128)S(1)} %get-tuple-element.12.own), custom_call_target="tpu_custom_call" | custom-call | flops 10000000000 | bytes 1536 | tf_op jit(solution)/shard_map/pallas_call | solution.py:169
  33.2 0.0 collective-permute-done.2.mate
  33.2 4.7 %shard_map.41 = f32[64,1536]{1,0:T(8,128)S(1)} custom-call(f32[1536,128]{1,0:T(8,128)S(1)} %collective-permute-done.other, f32[2312,128]{1,0:T(8,128)S(1)} %collective-permute-done.2.mate, f32[64,1536]{1,0:T(8,128)S(1)} %get-tuple-element.16.partial), custom_call_target="tpu_custom_call" | custom-call | flops 1000000000 | bytes 1536 | tf_op jit(solution)/shard_map/pallas_call | solution.py:169
  37.9 9.0 %collective-permute-start.3 = (f32[64,1536]{1,0:T(8,128)S(1)}, f32[64,1536]{1,0:T(8,128)S(1)}, u32[]{:S(2)}, u32[]{:S(2)}) collective-permute-start(f32[64,1536]{1,0:T(8,128)S(1)} %shard_map.41), channel_id=1, source_target_pairs={{510,0},{3,1},{0,2},{5,3},{2,4},{7,5},{4,6},{9,7},{6,8},{11,9},{8,... | collective-permute-start | bytes 1179656 | tf_op jit(solution)/shard_map/ppermute | solution.py:199
  46.9 0.0 collective-permute-done.1.other_vec
  47.0 5.7 %shard_map.40 = f32[64,1536]{1,0:T(8,128)S(1)} custom-call(bf16[1536,1536]{1,0:T(8,128)(2,1)S(1)} %get-tuple-element.13.tile_high, bf16[1536,1536]{1,0:T(8,128)(2,1)S(1)} %get-tuple-element.14.tile_low, f32[64,1536]{1,0:T(8,128)S(1)} %collective-permute-done.1.other_vec, f32[2312,128]{1,0:T(8,128)S(1)} %get-tuple-element.12.own, ...), custom_call_target="tpu_custom_call" | custom-call | flops 1000000000 | bytes 1536 | tf_op jit(solution)/shard_map/pallas_call | solution.py:169
  52.7 0.0 collective-permute-done.3
  52.7 0.8 %add_bitcast_fusion = f32[1536,64]{0,1:T(8,128)} fusion(f32[64,1536]{1,0:T(8,128)S(1)} %collective-permute-done.3, f32[64,1536]{1,0:T(8,128)S(1)} %get-tuple-element.11, f32[64,1536]{1,0:T(8,128)S(1)} %shard_map.40), kind=kLoop, calls=%fused_computation | loop fusion | flops 196608 | bytes 1572864 | tf_op jit(solution)/shard_map/transpose | solution.py:201
  (1 shorter events, 0.0 us)
Async XLA Ops:
  0.0 4.5 %copy-start = (f32[1536,128]{1,0:T(8,128)S(1)}, f32[1536,128]{1,0:T(8,128)}, u32[]{:S(2)}) copy-start(f32[1536,128]{1,0:T(8,128)} %pts.1) | copy-start | bytes 2359300
  0.0 4.5 %copy-start.1 = (f32[1536,64]{0,1:T(8,128)S(1)}, f32[1536,64]{0,1:T(8,128)}, u32[]{:S(2)}) copy-start(f32[1536,64]{0,1:T(8,128)} %param.5) | copy-start | bytes 1179652
  0.0 4.6 %copy-start.2 = (f32[128]{0:T(128)S(1)}, f32[128]{0:T(128)}, u32[]{:S(2)}) copy-start(f32[128]{0:T(128)} %param.4) | copy-start | bytes 1540
  0.0 26.4 %collective-permute-start = (f32[1536,128]{1,0:T(8,128)}, f32[1536,128]{1,0:T(8,128)S(1)}, u32[]{:S(2)}, u32[]{:S(2)}) collective-permute-start(f32[1536,128]{1,0:T(8,128)} %pts.1), channel_id=1, source_target_pairs={{0,510},{1,3},{2,0},{3,5},{4,2},{5,7},{6,4},{7,9},{8,6},{9,11},{10... | collective-permute-start | bytes 2359304 | tf_op jit(solution)/shard_map/ppermute | solution.py:184
  9.2 24.0 %collective-permute-start.2 = (f32[2312,128]{1,0:T(8,128)S(1)}, f32[2312,128]{1,0:T(8,128)S(1)}, u32[]{:S(2)}, u32[]{:S(2)}) collective-permute-start(f32[2312,128]{1,0:T(8,128)S(1)} %get-tuple-element.12.own), channel_id=1, source_target_pairs={{0,1},{1,0},{2,3},{3,2},{4,5},{5,4},{6,7},{7,6},{8,9},{9,8},{10,11... | collective-permute-start | bytes 3551240 | tf_op jit(solution)/shard_map/ppermute | solution.py:193
  24.3 22.6 %collective-permute-start.1 = (f32[64,1536]{1,0:T(8,128)S(1)}, f32[64,1536]{1,0:T(8,128)S(1)}, u32[]{:S(2)}, u32[]{:S(2)}) collective-permute-start(f32[64,1536]{1,0:T(8,128)S(1)} %get-tuple-element.15), channel_id=1, source_target_pairs={{0,510},{1,3},{2,0},{3,5},{4,2},{5,7},{6,4},{7,9},{8,6},{9,11},{10... | collective-permute-start | bytes 1179656 | tf_op jit(solution)/shard_map/ppermute | solution.py:194
  37.9 14.8 %collective-permute-start.3 = (f32[64,1536]{1,0:T(8,128)S(1)}, f32[64,1536]{1,0:T(8,128)S(1)}, u32[]{:S(2)}, u32[]{:S(2)}) collective-permute-start(f32[64,1536]{1,0:T(8,128)S(1)} %shard_map.41), channel_id=1, source_target_pairs={{510,0},{3,1},{0,2},{5,3},{2,4},{7,5},{4,6},{9,7},{6,8},{11,9},{8,... | collective-permute-start | bytes 1179656 | tf_op jit(solution)/shard_map/ppermute | solution.py:199

commit v2 on v1

--- a/solution.py
+++ b/solution.py
@@ -7,12 +7,15 @@
 from jax.experimental.pallas import tpu as pltpu
 from jax.sharding import PartitionSpec as P
 
-F32, BF16 = jnp.float32, jnp.bfloat16
+F32, BF16, F8 = jnp.float32, jnp.bfloat16, jnp.float8_e4m3fn
+TILE_SCALE, VEC_SCALE = 2.0**16, 256.0
 SUBLANES, LANES = 8, 128
 WIDTH = 768
 VMEM_LIMIT = 24 * 2**20
+MOST_FLOPS = 10**10
+LANE_FLOPS = 10**10
 SELF_FLOPS = 10**9
-VISIT_FLOPS = 10**10
+VISIT_FLOPS = 3 * 10**9
 ROOT_LOG2E = math.sqrt(math.log2(math.e))
 
 
@@ -61,17 +64,31 @@
     return jnp.concatenate([high, high, low, sq], axis=1)
 
 
-def split_vectors(vec_t):
-    return jnp.concatenate(split(vec_t), axis=0)
+def vector_parts(vec, axis, most=None):
+    if most is None:
+        most = jnp.max(jnp.abs(vec))
+    most = jnp.maximum(most, 1e-30)
+    coarse = (vec * (VEC_SCALE / most)).astype(F8)
+    return jnp.concatenate(split(vec), axis=axis), coarse, most / (VEC_SCALE * TILE_SCALE)
+
+
+def split_vectors(vec_t, most=None):
+    return vector_parts(vec_t, 0, most)
+
+
+def column_vectors(vec_t):
+    return vector_parts(vec_t.T, 1)
 
 
 def apply_strip(tile_high, tile_low, vec, rhs):
-    both = dot(vec, tile_high)
-    return both[:rhs] + both[rhs:] + dot(vec[:rhs], tile_low)
+    both = dot(vec[0], tile_high)
+    return both[:rhs] + both[rhs:] + dot(vec[1], tile_low) * vec[2]
 
 
 def tile_strip(rows, column):
-    return split(jnp.exp2(dot(rows, column, 1)))
+    tile = jnp.exp2(dot(rows, column, 1))
+    high = tile.astype(BF16)
+    return high, ((tile - high.astype(F32)) * TILE_SCALE).astype(F8)
 
 
 def strips(points):
@@ -109,13 +126,9 @@
         out[:, at] = apply_strip(high, low, vec, rhs)
 
 
-def from_columns(high, low, column_vec, rhs):
-    both = dot(high, column_vec)
-    return both[:, :rhs] + both[:, rhs:] + dot(low, column_vec[:, :rhs])
-
-
-def column_vectors(vec_t):
-    return jnp.concatenate(split(vec_t.T), axis=1)
+def from_columns(high, low, vec, at, rhs):
+    both = dot(high, vec[0][at, :])
+    return both[:, :rhs] + both[:, rhs:] + dot(low, vec[1][at, :]) * vec[2]
 
 
 def visit_kernel(other, own, back, tile_high, tile_low):
@@ -129,13 +142,18 @@
         high, low = tile_strip(rows, column[at, :])
         tile_high[:, at] = high
         tile_low[:, at] = low
-        added = from_columns(high, low, vec[at, :], rhs)
+        added = from_columns(high, low, vec, at, rhs)
         partial = added if partial is None else partial + added
     back[...] = partial.T
 
 
-def mate_kernel(other, mate, partial, back):
+def most_kernel(vec_t, after, out):
+    out[...] = jnp.full(out.shape, jnp.max(jnp.abs(vec_t[...])), F32)
+
+
+def mate_kernel(other, mate, partial, most, back, most_out):
     rhs, points = back.shape
+    most_out[...] = most[...]
     gain = unpack_gain(mate)
     rows = row_factor(mate[:points, :], gain)
     vec = split_vectors(unpack_vectors(mate, rhs, points))
@@ -145,10 +163,10 @@
         back[:, at] = partial[:, at] + apply_strip(high, low, vec, rhs)
 
 
-def own_kernel(tile_high, tile_low, other_vec, own, mate, out):
+def own_kernel(tile_high, tile_low, other_vec, most, own, mate, out):
     rhs, points = out.shape
     gain = unpack_gain(own)
-    vec = split_vectors(other_vec[...])
+    vec = split_vectors(other_vec[...], most[:1, :1])
     column = column_factor(own[:points, :], gain)
     rows = row_factor(mate[:points, :], gain)
     mate_vec = split_vectors(unpack_vectors(mate, rhs, points))
@@ -178,12 +196,12 @@
     gain = inv_scale[None, :]
     vec_t = vectors.T
     product = jax.ShapeDtypeStruct((rhs, rows), F32)
-    tile = jax.ShapeDtypeStruct((rows, rows), BF16)
+    tile, rest = [jax.ShapeDtypeStruct((rows, rows), kind) for kind in (BF16, F8)]
     packed = jax.ShapeDtypeStruct((rows + rhs * rows // LANES + SUBLANES, LANES), F32)
 
     visitor = lax.ppermute(points, "blk", ahead)
     lane_shape = jax.ShapeDtypeStruct((SUBLANES, LANES), jnp.int32)
-    lane = call(lane_kernel, lane_shape, flops=VISIT_FLOPS)
+    lane = call(lane_kernel, lane_shape, flops=LANE_FLOPS)
     total, own, vec_copy = call(
         self_kernel,
         (product, packed, product),
@@ -193,11 +211,17 @@
     mate = lax.ppermute(own, "blk", swap)
     visitor_vec = lax.ppermute(vec_copy, "blk", ahead)
     partial, high, low = call(
-        visit_kernel, (product, tile, tile), visitor, own, flops=VISIT_FLOPS
-    )
-    partial = call(mate_kernel, product, visitor, mate, partial, flops=SELF_FLOPS)
+        visit_kernel, (product, tile, rest), visitor, own, flops=VISIT_FLOPS
+    )
+    most_shape = jax.ShapeDtypeStruct((SUBLANES, LANES), F32)
+    most = call(most_kernel, most_shape, visitor_vec, partial, flops=MOST_FLOPS)
+    partial, most = call(
+        mate_kernel, (product, most_shape), visitor, mate, partial, most, flops=SELF_FLOPS
+    )
     returned = lax.ppermute(partial, "blk", back_home)
-    gained = call(own_kernel, product, high, low, visitor_vec, own, mate, flops=SELF_FLOPS)
+    gained = call(
+        own_kernel, product, *(high, low, visitor_vec, most, own, mate), flops=SELF_FLOPS
+    )
     return (total + gained + returned).T
 
 

time: 53.7 us -> 49.8 us (0.927)
  the two profiles are of different devices: /device:TPU:1 before, /device:TPU:6 now
where the time goes in v2:
time: 49.8 us; the launch traced here: 49.6 us
  starting transfers between devices  22.4 us (45%)
  Pallas kernels  21.3 us (43%)
  waiting for transfers between devices  4.9 us (10%)
  other arithmetic  0.82 us (2%)
    pallas_call x6, Pallas kernels, call(): pl.pallas_call(kernel, out_shape=outs, compiler_params=pltpu.CompilerPara...  21.3 us
    ppermute x1, starting transfers between devices, per_device(): visitor = lax.ppermute(points, 'blk', ahead)  14.2 us
    ppermute x1, waiting for transfers between devices, per_device(): returned = lax.ppermute(partial, 'blk', back_home)  4.89 us
    ppermute x1, starting transfers between devices, per_device(): returned = lax.ppermute(partial, 'blk', back_home)  3.13 us
    ppermute x1, starting transfers between devices, per_device(): visitor_vec = lax.ppermute(vec_copy, 'blk', ahead)  2.93 us
    ppermute x1, starting transfers between devices, per_device(): mate = lax.ppermute(own, 'blk', swap)  2.1 us
  transfers between devices with their start and end apart: 4, of which 1 were waited for; matrix products, arithmetic and copies ran while one was open for 0% of the time, Pallas kernels for 33%

profile of v2, /device:TPU:6, one launch (start us, length us, event | category | flops | bytes accessed | tf_op | source)
XLA Modules:
  0.0 49.6 jit_solution(13671119209834493668)
XLA Ops:
  0.0 0.0 copy-start
  0.0 0.0 copy-start.1
  0.0 0.0 copy-start.2
  0.0 14.2 %collective-permute-start = (f32[1536,128]{1,0:T(8,128)}, f32[1536,128]{1,0:T(8,128)S(1)}, u32[]{:S(2)}, u32[]{:S(2)}) collective-permute-start(f32[1536,128]{1,0:T(8,128)} %pts.1), channel_id=1, source_target_pairs={{0,510},{1,3},{2,0},{3,5},{4,2},{5,7},{6,4},{7,9},{8,6},{9,11},{10... | collective-permute-start | bytes 2359304 | tf_op jit(solution)/shard_map/ppermute | solution.py:202
  14.3 0.0 copy-done
  14.3 0.0 copy-done.1
  14.3 0.0 copy-done.2
  14.3 4.8 %shard_map.38 = (f32[64,1536]{1,0:T(8,128)S(1)}, f32[2312,128]{1,0:T(8,128)S(1)}, f32[64,1536]{1,0:T(8,128)S(1)}) custom-call(s32[8,128]{1,0:T(8,128)S(1)} %shard_map.37.lane, f32[1536,128]{1,0:T(8,128)S(1)} %copy-done, f32[64,1536]{1,0:T(8,128)S(1)} %bitcast.4, f32[1,128]{1,0:T(1,128)S(1)} %bitcast.5), custom_call_target="tpu_custom_call" | custom-call | flops 1000000000 | bytes 1536 | tf_op jit(solution)/shard_map/pallas_call | solution.py:187
  19.1 2.9 %collective-permute-start.1 = (f32[64,1536]{1,0:T(8,128)S(1)}, f32[64,1536]{1,0:T(8,128)S(1)}, u32[]{:S(2)}, u32[]{:S(2)}) collective-permute-start(f32[64,1536]{1,0:T(8,128)S(1)} %get-tuple-element.17), channel_id=1, source_target_pairs={{0,510},{1,3},{2,0},{3,5},{4,2},{5,7},{6,4},{7,9},{8,6},{9,11},{10... | collective-permute-start | bytes 1179656 | tf_op jit(solution)/shard_map/ppermute | solution.py:212
  22.0 2.1 %collective-permute-start.2 = (f32[2312,128]{1,0:T(8,128)S(1)}, f32[2312,128]{1,0:T(8,128)S(1)}, u32[]{:S(2)}, u32[]{:S(2)}) collective-permute-start(f32[2312,128]{1,0:T(8,128)S(1)} %get-tuple-element.14.own), channel_id=1, source_target_pairs={{0,1},{1,0},{2,3},{3,2},{4,5},{5,4},{6,7},{7,6},{8,9},{9,8},{10,11... | collective-permute-start | bytes 3551240 | tf_op jit(solution)/shard_map/ppermute | solution.py:211
  24.1 0.0 collective-permute-done.other
  24.2 5.5 %shard_map.39 = (f32[64,1536]{1,0:T(8,128)S(1)}, bf16[1536,1536]{1,0:T(8,128)(2,1)S(1)}, f8e4m3fn[1536,1536]{1,0:T(32,128)(4,1)S(1)}) custom-call(f32[1536,128]{1,0:T(8,128)S(1)} %collective-permute-done.other, f32[2312,128]{1,0:T(8,128)S(1)} %get-tuple-element.14.own), custom_call_target="tpu_custom_call" | custom-call | flops 3000000000 | bytes 1536 | tf_op jit(solution)/shard_map/pallas_call | solution.py:187
  29.6 0.0 collective-permute-done.1.vec_t.other_vec
  29.6 0.1 shard_map.40.most
  29.8 0.0 collective-permute-done.2.mate
  29.8 4.8 %shard_map.41 = (f32[64,1536]{1,0:T(8,128)S(1)}, f32[8,128]{1,0:T(8,128)S(1)}) custom-call(f32[1536,128]{1,0:T(8,128)S(1)} %collective-permute-done.other, f32[2312,128]{1,0:T(8,128)S(1)} %collective-permute-done.2.mate, f32[64,1536]{1,0:T(8,128)S(1)} %get-tuple-element.18.after.partial, f32[8,128]{1,0:T(8,128)S(1)} %shard_map.40.most), custom_call_target="tpu_custom_call" | custom-call | flops 1000000000 | bytes 1536 | tf_op jit(solution)/shard_map/pallas_call | solution.py:187
  34.6 3.1 %collective-permute-start.3 = (f32[64,1536]{1,0:T(8,128)S(1)}, f32[64,1536]{1,0:T(8,128)S(1)}, u32[]{:S(2)}, u32[]{:S(2)}) collective-permute-start(f32[64,1536]{1,0:T(8,128)S(1)} %get-tuple-element.20), channel_id=1, source_target_pairs={{510,0},{3,1},{0,2},{5,3},{2,4},{7,5},{4,6},{9,7},{6,8},{11,9},{8,... | collective-permute-start | bytes 1179656 | tf_op jit(solution)/shard_map/ppermute | solution.py:221
  37.7 6.1 %shard_map.42 = f32[64,1536]{1,0:T(8,128)S(1)} custom-call(bf16[1536,1536]{1,0:T(8,128)(2,1)S(1)} %get-tuple-element.15.tile_high, f8e4m3fn[1536,1536]{1,0:T(32,128)(4,1)S(1)} %get-tuple-element.16.tile_low, f32[64,1536]{1,0:T(8,128)S(1)} %collective-permute-done.1.vec_t.other_vec, f32[8,128]{1,0:T(8,128)S(1)} %get-tuple-element.19.most, ...), custom_call_target="tpu_custom_call" | custom-call | flops 1000000000 | bytes 1536 | tf_op jit(solution)/shard_map/pallas_call | solution.py:187
  43.9 4.9 %collective-permute-done.3 = f32[64,1536]{1,0:T(8,128)S(1)} collective-permute-done((f32[64,1536]{1,0:T(8,128)S(1)}, f32[64,1536]{1,0:T(8,128)S(1)}, u32[]{:S(2)}, u32[]{:S(2)}) %collective-permute-start.3) | collective-permute-done | bytes 393248 | tf_op jit(solution)/shard_map/ppermute | solution.py:221
  48.8 0.8 %add_bitcast_fusion = f32[1536,64]{0,1:T(8,128)} fusion(f32[64,1536]{1,0:T(8,128)S(1)} %collective-permute-done.3, f32[64,1536]{1,0:T(8,128)S(1)} %get-tuple-element.13, f32[64,1536]{1,0:T(8,128)S(1)} %shard_map.42), kind=kLoop, calls=%fused_computation | loop fusion | flops 196608 | bytes 1572864 | tf_op jit(solution)/shard_map/transpose | solution.py:225
  (1 shorter events, 0.0 us)
Async XLA Ops:
  0.0 14.3 %copy-start = (f32[1536,128]{1,0:T(8,128)S(1)}, f32[1536,128]{1,0:T(8,128)}, u32[]{:S(2)}) copy-start(f32[1536,128]{1,0:T(8,128)} %pts.1) | copy-start | bytes 2359300
  0.0 14.3 %copy-start.1 = (f32[1536,64]{0,1:T(8,128)S(1)}, f32[1536,64]{0,1:T(8,128)}, u32[]{:S(2)}) copy-start(f32[1536,64]{0,1:T(8,128)} %param.5) | copy-start | bytes 1179652
  0.0 14.3 %copy-start.2 = (f32[128]{0:T(128)S(1)}, f32[128]{0:T(128)}, u32[]{:S(2)}) copy-start(f32[128]{0:T(128)} %param.4) | copy-start | bytes 1540
  0.0 24.1 %collective-permute-start = (f32[1536,128]{1,0:T(8,128)}, f32[1536,128]{1,0:T(8,128)S(1)}, u32[]{:S(2)}, u32[]{:S(2)}) collective-permute-start(f32[1536,128]{1,0:T(8,128)} %pts.1), channel_id=1, source_target_pairs={{0,510},{1,3},{2,0},{3,5},{4,2},{5,7},{6,4},{7,9},{8,6},{9,11},{10... | collective-permute-start | bytes 2359304 | tf_op jit(solution)/shard_map/ppermute | solution.py:202
  19.1 10.5 %collective-permute-start.1 = (f32[64,1536]{1,0:T(8,128)S(1)}, f32[64,1536]{1,0:T(8,128)S(1)}, u32[]{:S(2)}, u32[]{:S(2)}) collective-permute-start(f32[64,1536]{1,0:T(8,128)S(1)} %get-tuple-element.17), channel_id=1, source_target_pairs={{0,510},{1,3},{2,0},{3,5},{4,2},{5,7},{6,4},{7,9},{8,6},{9,11},{10... | collective-permute-start | bytes 1179656 | tf_op jit(solution)/shard_map/ppermute | solution.py:212
  22.0 7.8 %collective-permute-start.2 = (f32[2312,128]{1,0:T(8,128)S(1)}, f32[2312,128]{1,0:T(8,128)S(1)}, u32[]{:S(2)}, u32[]{:S(2)}) collective-permute-start(f32[2312,128]{1,0:T(8,128)S(1)} %get-tuple-element.14.own), channel_id=1, source_target_pairs={{0,1},{1,0},{2,3},{3,2},{4,5},{5,4},{6,7},{7,6},{8,9},{9,8},{10,11... | collective-permute-start | bytes 3551240 | tf_op jit(solution)/shard_map/ppermute | solution.py:211
  34.6 14.2 %collective-permute-start.3 = (f32[64,1536]{1,0:T(8,128)S(1)}, f32[64,1536]{1,0:T(8,128)S(1)}, u32[]{:S(2)}, u32[]{:S(2)}) collective-permute-start(f32[64,1536]{1,0:T(8,128)S(1)} %get-tuple-element.20), channel_id=1, source_target_pairs={{510,0},{3,1},{0,2},{5,3},{2,4},{7,5},{4,6},{9,7},{6,8},{11,9},{8,... | collective-permute-start | bytes 1179656 | tf_op jit(solution)/shard_map/ppermute | solution.py:221

commit v3 on v2

--- a/solution.py
+++ b/solution.py
@@ -10,8 +10,8 @@
 F32, BF16, F8 = jnp.float32, jnp.bfloat16, jnp.float8_e4m3fn
 TILE_SCALE, VEC_SCALE = 2.0**16, 256.0
 SUBLANES, LANES = 8, 128
-WIDTH = 768
-VMEM_LIMIT = 24 * 2**20
+WIDTH = 1536
+VMEM_LIMIT = 36 * 2**20
 MOST_FLOPS = 10**10
 LANE_FLOPS = 10**10
 SELF_FLOPS = 10**9

time: 49.8 us -> 49.2 us (0.988)
  Pallas kernels: 21.3 us -> 19.8 us
  waiting for transfers between devices: 4.9 us -> 6.01 us
    pallas_call x6, Pallas kernels: 21.3 us -> 19.8 us  [call(): pl.pallas_call(kernel, out_shape=outs, compiler_params=pltpu.CompilerPara...]
    ppermute x1, waiting for transfers between devices: 4.89 us -> 5.78 us  [per_device(): returned = lax.ppermute(partial, 'blk', back_home)]
  transfers between devices with their start and end apart: 4 -> 4, of which waited for: 1 -> 2; matrix products, arithmetic and copies ran while one was open for 0% -> 0% of each run, Pallas kernels for 33% -> 31%
where the time goes in v3:
time: 49.2 us; the launch traced here: 49 us
  starting transfers between devices  22.2 us (45%)
  Pallas kernels  19.8 us (40%)
  waiting for transfers between devices  6.01 us (12%)
  other arithmetic  0.82 us (2%)
    pallas_call x6, Pallas kernels, call(): pl.pallas_call(kernel, out_shape=outs, compiler_params=pltpu.CompilerPara...  19.8 us
    ppermute x1, starting transfers between devices, per_device(): visitor = lax.ppermute(points, 'blk', ahead)  14.2 us
    ppermute x1, waiting for transfers between devices, per_device(): returned = lax.ppermute(partial, 'blk', back_home)  5.78 us
    ppermute x1, starting transfers between devices, per_device(): returned = lax.ppermute(partial, 'blk', back_home)  2.93 us
    ppermute x1, starting transfers between devices, per_device(): visitor_vec = lax.ppermute(vec_copy, 'blk', ahead)  2.92 us
    ppermute x1, starting transfers between devices, per_device(): mate = lax.ppermute(own, 'blk', swap)  2.1 us
  transfers between devices with their start and end apart: 4, of which 2 were waited for; matrix products, arithmetic and copies ran while one was open for 0% of the time, Pallas kernels for 31%

profile of v3, /device:TPU:6, one launch (start us, length us, event | category | flops | bytes accessed | tf_op | source)
XLA Modules:
  0.0 49.0 jit_solution(16063485047757647681)
XLA Ops:
  0.0 0.0 copy-start
  0.0 0.0 copy-start.1
  0.0 0.0 copy-start.2
  0.0 14.2 %collective-permute-start = (f32[1536,128]{1,0:T(8,128)}, f32[1536,128]{1,0:T(8,128)S(1)}, u32[]{:S(2)}, u32[]{:S(2)}) collective-permute-start(f32[1536,128]{1,0:T(8,128)} %pts.1), channel_id=1, source_target_pairs={{0,510},{1,3},{2,0},{3,5},{4,2},{5,7},{6,4},{7,9},{8,6},{9,11},{10... | collective-permute-start | bytes 2359304 | tf_op jit(solution)/shard_map/ppermute | solution.py:202
  14.3 0.0 copy-done
  14.3 0.0 copy-done.1
  14.3 0.0 copy-done.2
  14.3 4.5 %shard_map.38 = (f32[64,1536]{1,0:T(8,128)S(1)}, f32[2312,128]{1,0:T(8,128)S(1)}, f32[64,1536]{1,0:T(8,128)S(1)}) custom-call(s32[8,128]{1,0:T(8,128)S(1)} %shard_map.37.lane, f32[1536,128]{1,0:T(8,128)S(1)} %copy-done, f32[64,1536]{1,0:T(8,128)S(1)} %bitcast.4, f32[1,128]{1,0:T(1,128)S(1)} %bitcast.5), custom_call_target="tpu_custom_call" | custom-call | flops 1000000000 | bytes 1536 | tf_op jit(solution)/shard_map/pallas_call | solution.py:187
  18.8 2.9 %collective-permute-start.1 = (f32[64,1536]{1,0:T(8,128)S(1)}, f32[64,1536]{1,0:T(8,128)S(1)}, u32[]{:S(2)}, u32[]{:S(2)}) collective-permute-start(f32[64,1536]{1,0:T(8,128)S(1)} %get-tuple-element.17), channel_id=1, source_target_pairs={{0,510},{1,3},{2,0},{3,5},{4,2},{5,7},{6,4},{7,9},{8,6},{9,11},{10... | collective-permute-start | bytes 1179656 | tf_op jit(solution)/shard_map/ppermute | solution.py:212
  21.7 2.1 %collective-permute-start.2 = (f32[2312,128]{1,0:T(8,128)S(1)}, f32[2312,128]{1,0:T(8,128)S(1)}, u32[]{:S(2)}, u32[]{:S(2)}) collective-permute-start(f32[2312,128]{1,0:T(8,128)S(1)} %get-tuple-element.14.own), channel_id=1, source_target_pairs={{0,1},{1,0},{2,3},{3,2},{4,5},{5,4},{6,7},{7,6},{8,9},{9,8},{10,11... | collective-permute-start | bytes 3551240 | tf_op jit(solution)/shard_map/ppermute | solution.py:211
  23.9 0.2 collective-permute-done.other
  24.1 5.3 %shard_map.39 = (f32[64,1536]{1,0:T(8,128)S(1)}, bf16[1536,1536]{1,0:T(8,128)(2,1)S(1)}, f8e4m3fn[1536,1536]{1,0:T(32,128)(4,1)S(1)}) custom-call(f32[1536,128]{1,0:T(8,128)S(1)} %collective-permute-done.other, f32[2312,128]{1,0:T(8,128)S(1)} %get-tuple-element.14.own), custom_call_target="tpu_custom_call" | custom-call | flops 3000000000 | bytes 1536 | tf_op jit(solution)/shard_map/pallas_call | solution.py:187
  29.3 0.0 collective-permute-done.1.vec_t.other_vec
  29.3 0.1 shard_map.40.most
  29.5 0.0 collective-permute-done.2.mate
  29.5 4.4 %shard_map.41 = (f32[64,1536]{1,0:T(8,128)S(1)}, f32[8,128]{1,0:T(8,128)S(1)}) custom-call(f32[1536,128]{1,0:T(8,128)S(1)} %collective-permute-done.other, f32[2312,128]{1,0:T(8,128)S(1)} %collective-permute-done.2.mate, f32[64,1536]{1,0:T(8,128)S(1)} %get-tuple-element.18.after.partial, f32[8,128]{1,0:T(8,128)S(1)} %shard_map.40.most), custom_call_target="tpu_custom_call" | custom-call | flops 1000000000 | bytes 1536 | tf_op jit(solution)/shard_map/pallas_call | solution.py:187
  33.9 2.9 %collective-permute-start.3 = (f32[64,1536]{1,0:T(8,128)S(1)}, f32[64,1536]{1,0:T(8,128)S(1)}, u32[]{:S(2)}, u32[]{:S(2)}) collective-permute-start(f32[64,1536]{1,0:T(8,128)S(1)} %get-tuple-element.20), channel_id=1, source_target_pairs={{510,0},{3,1},{0,2},{5,3},{2,4},{7,5},{4,6},{9,7},{6,8},{11,9},{8,... | collective-permute-start | bytes 1179656 | tf_op jit(solution)/shard_map/ppermute | solution.py:221
  36.8 5.5 %shard_map.42 = f32[64,1536]{1,0:T(8,128)S(1)} custom-call(bf16[1536,1536]{1,0:T(8,128)(2,1)S(1)} %get-tuple-element.15.tile_high, f8e4m3fn[1536,1536]{1,0:T(32,128)(4,1)S(1)} %get-tuple-element.16.tile_low, f32[64,1536]{1,0:T(8,128)S(1)} %collective-permute-done.1.vec_t.other_vec, f32[8,128]{1,0:T(8,128)S(1)} %get-tuple-element.19.most, ...), custom_call_target="tpu_custom_call" | custom-call | flops 1000000000 | bytes 1536 | tf_op jit(solution)/shard_map/pallas_call | solution.py:187
  42.4 5.8 %collective-permute-done.3 = f32[64,1536]{1,0:T(8,128)S(1)} collective-permute-done((f32[64,1536]{1,0:T(8,128)S(1)}, f32[64,1536]{1,0:T(8,128)S(1)}, u32[]{:S(2)}, u32[]{:S(2)}) %collective-permute-start.3) | collective-permute-done | bytes 393248 | tf_op jit(solution)/shard_map/ppermute | solution.py:221
  48.2 0.8 %add_bitcast_fusion = f32[1536,64]{0,1:T(8,128)} fusion(f32[64,1536]{1,0:T(8,128)S(1)} %collective-permute-done.3, f32[64,1536]{1,0:T(8,128)S(1)} %get-tuple-element.13, f32[64,1536]{1,0:T(8,128)S(1)} %shard_map.42), kind=kLoop, calls=%fused_computation | loop fusion | flops 196608 | bytes 1572864 | tf_op jit(solution)/shard_map/transpose | solution.py:225
  (1 shorter events, 0.0 us)
Async XLA Ops:
  0.0 14.3 %copy-start = (f32[1536,128]{1,0:T(8,128)S(1)}, f32[1536,128]{1,0:T(8,128)}, u32[]{:S(2)}) copy-start(f32[1536,128]{1,0:T(8,128)} %pts.1) | copy-start | bytes 2359300
  0.0 14.3 %copy-start.1 = (f32[1536,64]{0,1:T(8,128)S(1)}, f32[1536,64]{0,1:T(8,128)}, u32[]{:S(2)}) copy-start(f32[1536,64]{0,1:T(8,128)} %param.5) | copy-start | bytes 1179652
  0.0 14.3 %copy-start.2 = (f32[128]{0:T(128)S(1)}, f32[128]{0:T(128)}, u32[]{:S(2)}) copy-start(f32[128]{0:T(128)} %param.4) | copy-start | bytes 1540
  0.0 24.1 %collective-permute-start = (f32[1536,128]{1,0:T(8,128)}, f32[1536,128]{1,0:T(8,128)S(1)}, u32[]{:S(2)}, u32[]{:S(2)}) collective-permute-start(f32[1536,128]{1,0:T(8,128)} %pts.1), channel_id=1, source_target_pairs={{0,510},{1,3},{2,0},{3,5},{4,2},{5,7},{6,4},{7,9},{8,6},{9,11},{10... | collective-permute-start | bytes 2359304 | tf_op jit(solution)/shard_map/ppermute | solution.py:202
  18.8 10.5 %collective-permute-start.1 = (f32[64,1536]{1,0:T(8,128)S(1)}, f32[64,1536]{1,0:T(8,128)S(1)}, u32[]{:S(2)}, u32[]{:S(2)}) collective-permute-start(f32[64,1536]{1,0:T(8,128)S(1)} %get-tuple-element.17), channel_id=1, source_target_pairs={{0,510},{1,3},{2,0},{3,5},{4,2},{5,7},{6,4},{7,9},{8,6},{9,11},{10... | collective-permute-start | bytes 1179656 | tf_op jit(solution)/shard_map/ppermute | solution.py:212
  21.7 7.8 %collective-permute-start.2 = (f32[2312,128]{1,0:T(8,128)S(1)}, f32[2312,128]{1,0:T(8,128)S(1)}, u32[]{:S(2)}, u32[]{:S(2)}) collective-permute-start(f32[2312,128]{1,0:T(8,128)S(1)} %get-tuple-element.14.own), channel_id=1, source_target_pairs={{0,1},{1,0},{2,3},{3,2},{4,5},{5,4},{6,7},{7,6},{8,9},{9,8},{10,11... | collective-permute-start | bytes 3551240 | tf_op jit(solution)/shard_map/ppermute | solution.py:211
  33.9 14.3 %collective-permute-start.3 = (f32[64,1536]{1,0:T(8,128)S(1)}, f32[64,1536]{1,0:T(8,128)S(1)}, u32[]{:S(2)}, u32[]{:S(2)}) collective-permute-start(f32[64,1536]{1,0:T(8,128)S(1)} %get-tuple-element.20), channel_id=1, source_target_pairs={{510,0},{3,1},{0,2},{5,3},{2,4},{7,5},{4,6},{9,7},{6,8},{11,9},{8,... | collective-permute-start | bytes 1179656 | tf_op jit(solution)/shard_map/ppermute | solution.py:221

commit v4 on v3

--- a/solution.py
+++ b/solution.py
@@ -30,38 +30,20 @@
 
 
 def split_points(points, gain):
-    scaled = points * (gain * ROOT_LOG2E)
-    high, low = split(scaled)
-    h, l = high.astype(F32), low.astype(F32)
-    half = -0.5 * jnp.sum(h * (h + 2.0 * l), axis=1, keepdims=True)
-    first = half.astype(BF16).astype(F32)
-    second = (half - first).astype(BF16).astype(F32)
-    third = half - first - second
-    return high, low, (first, second, third)
-
-
-def place(parts, ones_at, parts_at, points, lane):
-    ones = jnp.where((lane >= ones_at) & (lane < ones_at + 3), 1.0, 0.0)
-    out = jnp.broadcast_to(ones, (points, LANES))
-    for at, part in enumerate(parts):
-        out = jnp.where(lane == parts_at + at, part, out)
-    return out.astype(BF16)
-
-
-def lanes():
-    return lax.broadcasted_iota(jnp.int32, (1, LANES), 1)
-
-
-def row_factor(points, gain, lane=None):
-    high, low, parts = split_points(points, gain)
-    sq = place(parts, 3, 0, points.shape[0], lanes() if lane is None else lane)
-    return jnp.concatenate([high, low, high, sq], axis=1)
-
-
-def column_factor(points, gain, lane=None):
-    high, low, parts = split_points(points, gain)
-    sq = place(parts, 0, 3, points.shape[0], lanes() if lane is None else lane)
-    return jnp.concatenate([high, high, low, sq], axis=1)
+    high, low = split(points * (gain * ROOT_LOG2E))
+    whole = high.astype(F32) + low.astype(F32)
+    return high, low, -0.5 * jnp.sum(whole * whole, axis=1, keepdims=True)
+
+
+def row_factor(points, gain):
+    high, low, half = split_points(points, gain)
+    return jnp.concatenate([high, low, high, low], axis=1), half
+
+
+def column_factor(points, gain):
+    high, low, half = split_points(points, gain)
+    half = jnp.broadcast_to(half, points.shape).T[:1, :]
+    return jnp.concatenate([high, high, low, low], axis=1), half
 
 
 def vector_parts(vec, axis, most=None):
@@ -85,8 +67,9 @@
     return both[:rhs] + both[rhs:] + dot(vec[1], tile_low) * vec[2]
 
 
-def tile_strip(rows, column):
-    tile = jnp.exp2(dot(rows, column, 1))
+def tile_strip(rows, column, at):
+    cross = dot(rows[0], column[0][at, :], 1)
+    tile = jnp.exp2(cross + rows[1] + column[1][:, at])
     high = tile.astype(BF16)
     return high, ((tile - high.astype(F32)) * TILE_SCALE).astype(F8)
 
@@ -118,11 +101,11 @@
     end = points + rhs * points // LANES
     packed[end:, :] = jnp.broadcast_to(gain[...], (SUBLANES, LANES))
     vec_out[...] = vec_t[...]
-    column = column_factor(pts[...], gain[...], lane[:1, :])
-    rows = row_factor(pts[...], gain[...], lane[:1, :])
+    column = column_factor(pts[...], gain[...])
+    rows = row_factor(pts[...], gain[...])
     vec = split_vectors(vec_t[...])
     for at in strips(points):
-        high, low = tile_strip(rows, column[at, :])
+        high, low = tile_strip(rows, column, at)
         out[:, at] = apply_strip(high, low, vec, rhs)
 
 
@@ -139,7 +122,7 @@
     rows = row_factor(other[...], gain)
     partial = None
     for at in strips(points):
-        high, low = tile_strip(rows, column[at, :])
+        high, low = tile_strip(rows, column, at)
         tile_high[:, at] = high
         tile_low[:, at] = low
         added = from_columns(high, low, vec, at, rhs)
@@ -159,7 +142,7 @@
     vec = split_vectors(unpack_vectors(mate, rhs, points))
     column = column_factor(other[...], gain)
     for at in strips(points):
-        high, low = tile_strip(rows, column[at, :])
+        high, low = tile_strip(rows, column, at)
         back[:, at] = partial[:, at] + apply_strip(high, low, vec, rhs)
 
 
@@ -172,7 +155,7 @@
     mate_vec = split_vectors(unpack_vectors(mate, rhs, points))
     for at in strips(points):
         gained = apply_strip(tile_high[:, at], tile_low[:, at], vec, rhs)
-        high, low = tile_strip(rows, column[at, :])
+        high, low = tile_strip(rows, column, at)
         out[:, at] = gained + apply_strip(high, low, mate_vec, rhs)
 
 

time: 49.2 us -> 49.5 us (level)
  Pallas kernels: 19.8 us -> 20.3 us
  transfers between devices with their start and end apart: 4 -> 4, of which waited for: 2 -> 2; matrix products, arithmetic and copies ran while one was open for 0% -> 0% of each run, Pallas kernels for 31% -> 32%
where the time goes in v4:
time: 49.5 us; the launch traced here: 49.3 us
  starting transfers between devices  22.3 us (45%)
  Pallas kernels  20.3 us (41%)
  waiting for transfers between devices  5.75 us (12%)
  other arithmetic  0.82 us (2%)
    pallas_call x6, Pallas kernels, call(): pl.pallas_call(kernel, out_shape=outs, compiler_params=pltpu.CompilerPara...  20.3 us
    ppermute x1, starting transfers between devices, per_device(): visitor = lax.ppermute(points, 'blk', ahead)  14.2 us
    ppermute x1, waiting for transfers between devices, per_device(): returned = lax.ppermute(partial, 'blk', back_home)  5.63 us
    ppermute x1, starting transfers between devices, per_device(): returned = lax.ppermute(partial, 'blk', back_home)  3.07 us
    ppermute x1, starting transfers between devices, per_device(): visitor_vec = lax.ppermute(vec_copy, 'blk', ahead)  2.89 us
    ppermute x1, starting transfers between devices, per_device(): mate = lax.ppermute(own, 'blk', swap)  2.1 us
  transfers between devices with their start and end apart: 4, of which 2 were waited for; matrix products, arithmetic and copies ran while one was open for 0% of the time, Pallas kernels for 32%

profile of v4, /device:TPU:6, one launch (start us, length us, event | category | flops | bytes accessed | tf_op | source)
XLA Modules:
  0.0 49.3 jit_solution(1532085041068305025)
XLA Ops:
  0.0 0.0 copy-start
  0.0 0.0 copy-start.1
  0.0 0.0 copy-start.2
  0.0 14.2 %collective-permute-start = (f32[1536,128]{1,0:T(8,128)}, f32[1536,128]{1,0:T(8,128)S(1)}, u32[]{:S(2)}, u32[]{:S(2)}) collective-permute-start(f32[1536,128]{1,0:T(8,128)} %pts.1), channel_id=1, source_target_pairs={{0,510},{1,3},{2,0},{3,5},{4,2},{5,7},{6,4},{7,9},{8,6},{9,11},{10... | collective-permute-start | bytes 2359304 | tf_op jit(solution)/shard_map/ppermute | solution.py:185
  14.3 0.0 copy-done
  14.3 0.0 copy-done.1
  14.3 0.0 copy-done.2
  14.3 4.6 %shard_map.38 = (f32[64,1536]{1,0:T(8,128)S(1)}, f32[2312,128]{1,0:T(8,128)S(1)}, f32[64,1536]{1,0:T(8,128)S(1)}) custom-call(s32[8,128]{1,0:T(8,128)S(1)} %shard_map.37.lane, f32[1536,128]{1,0:T(8,128)S(1)} %copy-done, f32[64,1536]{1,0:T(8,128)S(1)} %bitcast.4, f32[1,128]{1,0:T(1,128)S(1)} %bitcast.5), custom_call_target="tpu_custom_call" | custom-call | flops 1000000000 | bytes 1536 | tf_op jit(solution)/shard_map/pallas_call | solution.py:170
  18.9 2.9 %collective-permute-start.1 = (f32[64,1536]{1,0:T(8,128)S(1)}, f32[64,1536]{1,0:T(8,128)S(1)}, u32[]{:S(2)}, u32[]{:S(2)}) collective-permute-start(f32[64,1536]{1,0:T(8,128)S(1)} %get-tuple-element.17), channel_id=1, source_target_pairs={{0,510},{1,3},{2,0},{3,5},{4,2},{5,7},{6,4},{7,9},{8,6},{9,11},{10... | collective-permute-start | bytes 1179656 | tf_op jit(solution)/shard_map/ppermute | solution.py:195
  21.8 2.1 %collective-permute-start.2 = (f32[2312,128]{1,0:T(8,128)S(1)}, f32[2312,128]{1,0:T(8,128)S(1)}, u32[]{:S(2)}, u32[]{:S(2)}) collective-permute-start(f32[2312,128]{1,0:T(8,128)S(1)} %get-tuple-element.14.own), channel_id=1, source_target_pairs={{0,1},{1,0},{2,3},{3,2},{4,5},{5,4},{6,7},{7,6},{8,9},{9,8},{10,11... | collective-permute-start | bytes 3551240 | tf_op jit(solution)/shard_map/ppermute | solution.py:194
  24.0 0.1 collective-permute-done.other
  24.1 5.4 %shard_map.39 = (f32[64,1536]{1,0:T(8,128)S(1)}, bf16[1536,1536]{1,0:T(8,128)(2,1)S(1)}, f8e4m3fn[1536,1536]{1,0:T(32,128)(4,1)S(1)}) custom-call(f32[1536,128]{1,0:T(8,128)S(1)} %collective-permute-done.other, f32[2312,128]{1,0:T(8,128)S(1)} %get-tuple-element.14.own), custom_call_target="tpu_custom_call" | custom-call | flops 3000000000 | bytes 1536 | tf_op jit(solution)/shard_map/pallas_call | solution.py:170
  29.5 0.0 collective-permute-done.1.vec_t.other_vec
  29.5 0.1 shard_map.40.most
  29.7 0.0 collective-permute-done.2.mate
  29.7 4.5 %shard_map.41 = (f32[64,1536]{1,0:T(8,128)S(1)}, f32[8,128]{1,0:T(8,128)S(1)}) custom-call(f32[1536,128]{1,0:T(8,128)S(1)} %collective-permute-done.other, f32[2312,128]{1,0:T(8,128)S(1)} %collective-permute-done.2.mate, f32[64,1536]{1,0:T(8,128)S(1)} %get-tuple-element.18.after.partial, f32[8,128]{1,0:T(8,128)S(1)} %shard_map.40.most), custom_call_target="tpu_custom_call" | custom-call | flops 1000000000 | bytes 1536 | tf_op jit(solution)/shard_map/pallas_call | solution.py:170
  34.2 3.1 %collective-permute-start.3 = (f32[64,1536]{1,0:T(8,128)S(1)}, f32[64,1536]{1,0:T(8,128)S(1)}, u32[]{:S(2)}, u32[]{:S(2)}) collective-permute-start(f32[64,1536]{1,0:T(8,128)S(1)} %get-tuple-element.20), channel_id=1, source_target_pairs={{510,0},{3,1},{0,2},{5,3},{2,4},{7,5},{4,6},{9,7},{6,8},{11,9},{8,... | collective-permute-start | bytes 1179656 | tf_op jit(solution)/shard_map/ppermute | solution.py:204
  37.3 5.5 %shard_map.42 = f32[64,1536]{1,0:T(8,128)S(1)} custom-call(bf16[1536,1536]{1,0:T(8,128)(2,1)S(1)} %get-tuple-element.15.tile_high, f8e4m3fn[1536,1536]{1,0:T(32,128)(4,1)S(1)} %get-tuple-element.16.tile_low, f32[64,1536]{1,0:T(8,128)S(1)} %collective-permute-done.1.vec_t.other_vec, f32[8,128]{1,0:T(8,128)S(1)} %get-tuple-element.19.most, ...), custom_call_target="tpu_custom_call" | custom-call | flops 1000000000 | bytes 1536 | tf_op jit(solution)/shard_map/pallas_call | solution.py:170
  42.8 5.6 %collective-permute-done.3 = f32[64,1536]{1,0:T(8,128)S(1)} collective-permute-done((f32[64,1536]{1,0:T(8,128)S(1)}, f32[64,1536]{1,0:T(8,128)S(1)}, u32[]{:S(2)}, u32[]{:S(2)}) %collective-permute-start.3) | collective-permute-done | bytes 393248 | tf_op jit(solution)/shard_map/ppermute | solution.py:204
  48.5 0.8 %add_bitcast_fusion = f32[1536,64]{0,1:T(8,128)} fusion(f32[64,1536]{1,0:T(8,128)S(1)} %collective-permute-done.3, f32[64,1536]{1,0:T(8,128)S(1)} %get-tuple-element.13, f32[64,1536]{1,0:T(8,128)S(1)} %shard_map.42), kind=kLoop, calls=%fused_computation | loop fusion | flops 196608 | bytes 1572864 | tf_op jit(solution)/shard_map/transpose | solution.py:208
  (1 shorter events, 0.0 us)
Async XLA Ops:
  0.0 14.3 %copy-start = (f32[1536,128]{1,0:T(8,128)S(1)}, f32[1536,128]{1,0:T(8,128)}, u32[]{:S(2)}) copy-start(f32[1536,128]{1,0:T(8,128)} %pts.1) | copy-start | bytes 2359300
  0.0 14.3 %copy-start.1 = (f32[1536,64]{0,1:T(8,128)S(1)}, f32[1536,64]{0,1:T(8,128)}, u32[]{:S(2)}) copy-start(f32[1536,64]{0,1:T(8,128)} %param.5) | copy-start | bytes 1179652
  0.0 14.3 %copy-start.2 = (f32[128]{0:T(128)S(1)}, f32[128]{0:T(128)}, u32[]{:S(2)}) copy-start(f32[128]{0:T(128)} %param.4) | copy-start | bytes 1540
  0.0 24.1 %collective-permute-start = (f32[1536,128]{1,0:T(8,128)}, f32[1536,128]{1,0:T(8,128)S(1)}, u32[]{:S(2)}, u32[]{:S(2)}) collective-permute-start(f32[1536,128]{1,0:T(8,128)} %pts.1), channel_id=1, source_target_pairs={{0,510},{1,3},{2,0},{3,5},{4,2},{5,7},{6,4},{7,9},{8,6},{9,11},{10... | collective-permute-start | bytes 2359304 | tf_op jit(solution)/shard_map/ppermute | solution.py:185
  18.9 10.5 %collective-permute-start.1 = (f32[64,1536]{1,0:T(8,128)S(1)}, f32[64,1536]{1,0:T(8,128)S(1)}, u32[]{:S(2)}, u32[]{:S(2)}) collective-permute-start(f32[64,1536]{1,0:T(8,128)S(1)} %get-tuple-element.17), channel_id=1, source_target_pairs={{0,510},{1,3},{2,0},{3,5},{4,2},{5,7},{6,4},{7,9},{8,6},{9,11},{10... | collective-permute-start | bytes 1179656 | tf_op jit(solution)/shard_map/ppermute | solution.py:195
  21.8 7.8 %collective-permute-start.2 = (f32[2312,128]{1,0:T(8,128)S(1)}, f32[2312,128]{1,0:T(8,128)S(1)}, u32[]{:S(2)}, u32[]{:S(2)}) collective-permute-start(f32[2312,128]{1,0:T(8,128)S(1)} %get-tuple-element.14.own), channel_id=1, source_target_pairs={{0,1},{1,0},{2,3},{3,2},{4,5},{5,4},{6,7},{7,6},{8,9},{9,8},{10,11... | collective-permute-start | bytes 3551240 | tf_op jit(solution)/shard_map/ppermute | solution.py:194
  34.2 14.2 %collective-permute-start.3 = (f32[64,1536]{1,0:T(8,128)S(1)}, f32[64,1536]{1,0:T(8,128)S(1)}, u32[]{:S(2)}, u32[]{:S(2)}) collective-permute-start(f32[64,1536]{1,0:T(8,128)S(1)} %get-tuple-element.20), channel_id=1, source_target_pairs={{510,0},{3,1},{0,2},{5,3},{2,4},{7,5},{4,6},{9,7},{6,8},{11,9},{8,... | collective-permute-start | bytes 1179656 | tf_op jit(solution)/shard_map/ppermute | solution.py:204
